TPU v7x, 32 devices: a whole 2x2x4 slice. The times are simulated.
32 devices in a mesh: px: 4 (over z), py: 8 (over y, x, core).
Axes of the slice: x: 2, y: 2, z: 4, core: 2. Of those that a mesh axis runs over, the one named last changes fastest.
Arguments:
- fractions: float32 [1024, 3, 128], P(('px', 'py')), may hold values from 0 to 1
- charge: float32 [1024, 128], P(('px', 'py')), may hold values from -4 to 4
- cell_index: int32 [1024, 128], P(('px', 'py')), may hold values from 0 to 524287
- destination: int32 [1024, 1], P(('px', 'py')), may hold values from 0 to 7; in each aligned block of 32 rows (0 to 31, 32 to 63, ...) at most 6 rows name the same one
- live_blocks: int32 [32], P(('px', 'py')), may hold values from 16 to 32, as said below
Outputs:
- forces: float32 [1024, 3, 128], P(('px', 'py'))
Inputs may be any that keep to these rules, and one draw needn't show every extreme that they name: `destination`: in the rows of one device no value is named by more than 6 blocks, a bound that some block reaches. `live_blocks`: some domain has all 32 slots occupied in every draw.
All inputs are finite; a program needn't handle non-finite values.
Results may differ from a plain program's by a relative error of at most 0.0003.
Values sent between devices are 32-bit elements; how exact they have to be, the bound alone decides.
A program may use at most 128 MiB of HBM per device.

v0:
```python
import math

import jax
import jax.numpy as jnp
from jax import lax
from jax.sharding import PartitionSpec as P

K = 256


EWALD_GAIN = 4.0
EWALD_BETA = 0.6
SPLINE_SUMS = (1.0 / 120.0, 26.0 / 120.0, 66.0 / 120.0, 26.0 / 120.0, 1.0 / 120.0)
HIGHEST = lax.Precision.HIGHEST


def swapped(block, axis, bit):
    count = lax.axis_size(axis)
    route = []
    for low in range(count):
        high = low | 1 << bit
        if high != low and high < count:
            route += [(low, high), (high, low)]
    return lax.ppermute(block, axis, route)


def from_behind(value, axis, steps):
    count = lax.axis_size(axis)
    pairs = [(source, (source + steps) % count) for source in range(count)]
    return lax.ppermute(value, axis, pairs)


def spline_six(u):
    older_values = [1.0 - u, u]
    slopes = []
    for spline_order in range(3, 7):
        newer_values = []
        for k in range(spline_order):
            from_left = older_values[k - 1] if k >= 1 else jnp.zeros_like(u)
            from_right = older_values[k] if k <= spline_order - 2 else jnp.zeros_like(u)
            newer_values.append(
                ((u + (spline_order - 1 - k)) * from_left + (k + 1 - u) * from_right)
                * (1.0 / (spline_order - 1))
            )
        if spline_order == 6:
            slopes = [
                (older_values[k - 1] if k >= 1 else jnp.zeros_like(u))
                - (older_values[k] if k <= 4 else jnp.zeros_like(u))
                for k in range(6)
            ]
        older_values = newer_values
    return (older_values, slopes)


def modulus(wave, extent):
    cos_sum = jnp.zeros(wave.shape, jnp.float32)
    sin_sum = jnp.zeros(wave.shape, jnp.float32)
    for j, value in enumerate(SPLINE_SUMS):
        angle = 2.0 * math.pi / extent * (wave * j % extent).astype(jnp.float32)
        cos_sum = cos_sum + value * jnp.cos(angle)
        sin_sum = sin_sum + value * jnp.sin(angle)
    return 1.0 / (cos_sum * cos_sum + sin_sum * sin_sum)


def influence(wave_x, wave_y, wave_z, extent):
    folded_x = jnp.where(2 * wave_x < extent, wave_x, wave_x - extent).astype(jnp.float32) / extent
    folded_y = jnp.where(2 * wave_y < extent, wave_y, wave_y - extent).astype(jnp.float32) / extent
    folded_z = jnp.where(2 * wave_z < extent, wave_z, wave_z - extent).astype(jnp.float32) / extent
    squared = folded_x * folded_x + folded_y * folded_y + folded_z * folded_z
    safe_squared = jnp.where(squared > 0, squared, 1.0)
    value = (
        EWALD_GAIN
        * jnp.exp(-(math.pi * math.pi) * squared / (EWALD_BETA * EWALD_BETA))
        / safe_squared
    )
    value = value * modulus(wave_x, extent) * modulus(wave_y, extent) * modulus(wave_z, extent)
    return jnp.where(squared > 0, value, 0.0)


def wave_tables(extent):
    steps = jnp.arange(extent, dtype=jnp.int32)
    product = steps[:, None] * steps[None, :] % extent
    angle = 2.0 * math.pi / extent * product.astype(jnp.float32)
    return (jnp.cos(angle), jnp.sin(angle))


def local_forward(start, count, parts):
    outputs = jnp.arange(count, dtype=jnp.int32)[:, None]
    inputs = jnp.arange(count, dtype=jnp.int32)[None, :]
    total = parts * count
    product = inputs * (start + parts * outputs) % total
    angle = -2.0 * math.pi / total * product.astype(jnp.float32)
    return (jnp.cos(angle), jnp.sin(angle))


def reverse_bits(index, count_bits):
    result = jnp.zeros((), jnp.int32)
    for b in range(count_bits):
        result = result + ((index >> b & 1) << count_bits - 1 - b)
    return result


def mix_rows(spectrum, mat_cos, mat_sin):

    def apply_matrix(matrix, values):
        return jnp.einsum("sm,myz->syz", matrix, values, precision=HIGHEST)

    real_part, imag_part = (spectrum[0], spectrum[1])
    return jnp.stack(
        [
            apply_matrix(mat_cos, real_part) - apply_matrix(mat_sin, imag_part),
            apply_matrix(mat_cos, imag_part) + apply_matrix(mat_sin, real_part),
        ]
    )


def mix_columns(spectrum, mat_cos, mat_sin):

    def apply_matrix(matrix, values):
        return jnp.einsum("sm,xmz->xsz", matrix, values, precision=HIGHEST)

    real_part, imag_part = (spectrum[0], spectrum[1])
    return jnp.stack(
        [
            apply_matrix(mat_cos, real_part) - apply_matrix(mat_sin, imag_part),
            apply_matrix(mat_cos, imag_part) + apply_matrix(mat_sin, real_part),
        ]
    )


def swap_rows(spectrum, bit_number):
    return swapped(spectrum, "px", bit_number)


def swap_columns(spectrum, bit_number):
    return swapped(spectrum, "py", bit_number)


def butterfly_section(spectrum, index, bit_number, inverse, exchanger):
    upper = index >> bit_number & 1 == 1
    lower = (index & (1 << bit_number) - 1).astype(jnp.float32)
    angle = -2.0 * math.pi / 2 ** (bit_number + 1) * lower
    turn_cos = jnp.cos(angle)
    turn_sin = jnp.sin(angle)
    real_part, imag_part = (spectrum[0], spectrum[1])
    if inverse:
        turned = jnp.stack(
            [
                turn_cos * real_part + turn_sin * imag_part,
                turn_cos * imag_part - turn_sin * real_part,
            ]
        )
        own_value = jnp.where(upper, turned, spectrum)
        partner = exchanger(own_value, bit_number)
        return jnp.where(upper, partner - own_value, own_value + partner)
    partner = exchanger(spectrum, bit_number)
    diff_real = partner[0] - real_part
    diff_imag = partner[1] - imag_part
    turned = jnp.stack(
        [turn_cos * diff_real - turn_sin * diff_imag, turn_sin * diff_real + turn_cos * diff_imag]
    )
    return jnp.where(upper, turned, spectrum + partner)


def place_table(base, values, span):
    atoms_count = base.shape[0]
    slots_index = jnp.arange(span, dtype=jnp.int32)[:, None]
    table = jnp.zeros((span, atoms_count), jnp.float32)
    for k in range(6):
        table = table + jnp.where(slots_index == (base + k)[None, :], values[k][None, :], 0.0)
    return table


def place_depth(base, values, extent):
    depth_index = jnp.arange(extent, dtype=jnp.int32)[None, :]
    table = jnp.zeros((base.shape[0], extent), jnp.float32)
    for k in range(6):
        table = table + jnp.where(
            depth_index == ((base + k) % extent)[:, None], values[k][:, None], 0.0
        )
    return table


def per_device(fractions, charge, cell_index, destination, live_blocks):
    rows_dev = lax.axis_size("px")
    cols_dev = lax.axis_size("py")
    span_x = K // rows_dev
    span_y = K // cols_dev
    blocks = charge.shape[0]
    width = charge.shape[1]
    capacity = max(2, 3 * blocks // (2 * cols_dev))
    slots = cols_dev * capacity
    group_blocks = 4
    groups = slots // group_blocks
    atoms_group = group_blocks * width
    alive = (jnp.arange(blocks, dtype=jnp.int32) < live_blocks[0]).astype(jnp.float32)
    target = destination[:, 0]
    matches = (target[:, None] == jnp.arange(cols_dev, dtype=jnp.int32)[None, :]).astype(jnp.int32)
    earlier = jnp.cumsum(matches, axis=0) - matches
    position = jnp.sum(earlier * matches, axis=1)
    slot_of = target * capacity + position
    picked = (slot_of[None, :] == jnp.arange(slots, dtype=jnp.int32)[:, None]).astype(jnp.int32)
    source_block = jnp.sum(picked * jnp.arange(blocks, dtype=jnp.int32)[None, :], axis=1)
    used = jnp.sum(picked, axis=1).astype(jnp.float32)
    payload = jnp.concatenate(
        [
            fractions,
            (charge * alive[:, None])[:, None, :],
            cell_index.astype(jnp.float32)[:, None, :],
        ],
        axis=1,
    )
    outgoing = (jnp.take(payload, source_block, axis=0) * used[:, None, None]).reshape(
        cols_dev, capacity, 5, width
    )
    arrived = lax.all_to_all(outgoing, "py", split_axis=0, concat_axis=0, tiled=True)
    grouped = (
        arrived.reshape(groups, group_blocks, 5, width)
        .transpose(0, 2, 1, 3)
        .reshape(groups, 5, atoms_group)
    )

    def deposit(charge_grid, group):
        cell_value = group[4].astype(jnp.int32)
        base_x = cell_value // (span_y * K)
        base_y = cell_value // K % span_y
        base_z = cell_value % K
        splines_x, slopes_x = spline_six(group[0])
        splines_y, slopes_y = spline_six(group[1])
        splines_z, slopes_z = spline_six(group[2])
        table_x = place_table(base_x, splines_x, span_x + 5)
        slope_x = place_table(base_x, slopes_x, span_x + 5)
        table_y = place_table(base_y, splines_y, span_y + 5)
        slope_y = place_table(base_y, slopes_y, span_y + 5)
        table_z = place_depth(base_z, splines_z, K)
        slope_z = place_depth(base_z, slopes_z, K)
        outer_table = (table_x[:, None, :] * table_y[None, :, :]).reshape(-1, atoms_group)
        charge_grid = charge_grid + jnp.dot(
            outer_table, table_z * group[3][:, None], precision=HIGHEST
        )
        return (charge_grid, (table_x, slope_x, table_y, slope_y, table_z, slope_z, group[3]))

    start_grid = jnp.zeros(((span_x + 5) * (span_y + 5), K), jnp.float32)
    extended, stored = lax.scan(deposit, start_grid, grouped)
    extended = extended.reshape(span_x + 5, span_y + 5, K)
    moved_rows = from_behind(extended[span_x:], "px", 1)
    extended = jnp.concatenate([extended[:5] + moved_rows, extended[5:span_x]], axis=0)
    moved_cols = from_behind(extended[:, span_y:], "py", 1)
    charge_grid = jnp.concatenate([extended[:, :5] + moved_cols, extended[:, 5:span_y]], axis=1)
    depth_cos, depth_sin = wave_tables(K)
    flat_grid = charge_grid.reshape(span_x * span_y, K)
    spectrum = jnp.stack(
        [
            jnp.dot(flat_grid, depth_cos, precision=HIGHEST),
            -jnp.dot(flat_grid, depth_sin, precision=HIGHEST),
        ]
    ).reshape(2, span_x, span_y, K)
    index_x = lax.axis_index("px")
    index_y = lax.axis_index("py")
    bits_x = rows_dev.bit_length() - 1
    bits_y = cols_dev.bit_length() - 1
    start_x = reverse_bits(index_x, bits_x)
    start_y = reverse_bits(index_y, bits_y)
    for bit_number in reversed(range(bits_y)):
        spectrum = butterfly_section(spectrum, index_y, bit_number, False, swap_columns)
    column_cos, column_sin = local_forward(start_y, span_y, cols_dev)
    spectrum = mix_columns(spectrum, column_cos, column_sin)
    wave_y = start_y + cols_dev * jnp.arange(span_y, dtype=jnp.int32)
    wave_z = jnp.arange(K, dtype=jnp.int32)
    for bit_number in reversed(range(bits_x)):
        spectrum = butterfly_section(spectrum, index_x, bit_number, False, swap_rows)
    row_cos, row_sin = local_forward(start_x, span_x, rows_dev)
    spectrum = mix_rows(spectrum, row_cos, row_sin)
    wave_x = start_x + rows_dev * jnp.arange(span_x, dtype=jnp.int32)
    kernel = influence(wave_x[:, None, None], wave_y[None, :, None], wave_z[None, None, :], K) * (
        1.0 / float(K**3)
    )
    spectrum = spectrum * kernel[None]
    spectrum = mix_rows(spectrum, row_cos.T, -row_sin.T)
    for bit_number in range(bits_x):
        spectrum = butterfly_section(spectrum, index_x, bit_number, True, swap_rows)
    spectrum = mix_columns(spectrum, column_cos.T, -column_sin.T)
    for bit_number in range(bits_y):
        spectrum = butterfly_section(spectrum, index_y, bit_number, True, swap_columns)
    real_flat = spectrum[0].reshape(span_x * span_y, K)
    imag_flat = spectrum[1].reshape(span_x * span_y, K)
    potential = (
        jnp.dot(real_flat, depth_cos, precision=HIGHEST)
        - jnp.dot(imag_flat, depth_sin, precision=HIGHEST)
    ).reshape(span_x, span_y, K)
    lower_rows = from_behind(potential[:5], "px", -1)
    potential = jnp.concatenate([potential, lower_rows], axis=0)
    lower_cols = from_behind(potential[:, :5], "py", -1)
    potential = jnp.concatenate([potential, lower_cols], axis=1).reshape(-1, K)

    def pull(carry, tables):
        table_x, slope_x, table_y, slope_y, table_z, slope_z, amounts = tables
        stacked = jnp.stack(
            [
                table_x[:, None, :] * table_y[None, :, :],
                slope_x[:, None, :] * table_y[None, :, :],
                table_x[:, None, :] * slope_y[None, :, :],
            ]
        ).reshape(3, -1, atoms_group)
        sampled = jnp.einsum("cga,gz->caz", stacked, potential, precision=HIGHEST)
        force_x = -amounts * jnp.sum(sampled[1] * table_z, axis=1)
        force_y = -amounts * jnp.sum(sampled[2] * table_z, axis=1)
        force_z = -amounts * jnp.sum(sampled[0] * slope_z, axis=1)
        return (carry, jnp.stack([force_x, force_y, force_z]))

    _, pulled = lax.scan(pull, jnp.zeros((), jnp.float32), stored)
    pulled = (
        pulled.reshape(groups, 3, group_blocks, width)
        .transpose(0, 2, 1, 3)
        .reshape(cols_dev, capacity, 3, width)
    )
    returned = lax.all_to_all(pulled, "py", split_axis=0, concat_axis=0, tiled=True).reshape(
        slots, 3, width
    )
    return jnp.take(returned, slot_of, axis=0) * alive[:, None, None]


def solution(mesh):
    placed = (
        P(("px", "py"), None, None),
        P(("px", "py"), None),
        P(("px", "py"), None),
        P(("px", "py"), None),
        P(("px", "py")),
    )
    return jax.shard_map(
        per_device,
        mesh=mesh,
        in_specs=placed,
        out_specs=P(("px", "py"), None, None),
        check_vma=False,
    )
```

profile of v0, /device:TPU:0, one launch (start us, length us, event | category | flops | bytes accessed | tf_op | source)
XLA Modules:
  0.0 2037.1 jit_solution(7181257462529953207)
XLA Ops:
  18.2 323.6 %while.39 = (s32[]{:T(128)}, f32[2553,256]{1,0:T(8,128)S(1)}, f32[12,69,512]{2,1,0:T(8,128)}, f32[12,69,512]{2,1,0:T(8,128)}, f32[12,37,512]{2,1,0:T(8,128)}, /*...) while((s32[]{:T(128)}, f32[2553,256]{1,0:T(8,128)S(1)}, ...), condition=%wide.region_5.6_spmd.clone, body=%wide.region_4.5_spmd.clone.sunk | while | flops 4028009472 | bytes 28529896 | solution.py:244
  28.0 8.7 convolution_add_fusion.2
  55.0 8.7 convolution_add_fusion.2
  81.9 8.7 convolution_add_fusion.2
  108.9 8.7 convolution_add_fusion.2
  135.9 8.7 convolution_add_fusion.2
  162.8 8.7 convolution_add_fusion.2
  189.8 8.7 convolution_add_fusion.2
  216.7 8.7 convolution_add_fusion.2
  243.7 8.7 convolution_add_fusion.2
  270.7 8.7 convolution_add_fusion.2
  297.6 8.7 convolution_add_fusion.2
  324.6 8.7 convolution_add_fusion.2
  350.7 9.5 collective-permute-done.1
  369.6 89.4 %collective-permute-done.2 = f32[2,64,32,256]{3,2,1,0:T(8,128)} collective-permute-done((f32[2,64,32,256]{3,2,1,0:T(8,128)}, f32[2,64,32,256]{3,2,1,0:T(8,128)}, u32[]{:S(2)}, u32[]{:S(2)}) %collective-permute-start.2) | collective-permute-done | bytes 4194336 | tf_op jit(solution)/shard_map/ppermute | solution.py:24
  462.9 7.2 maximum_select_fusion
  471.7 89.0 %collective-permute-done.3 = f32[2,64,32,256]{3,2,1,0:T(8,128)} collective-permute-done((f32[2,64,32,256]{3,2,1,0:T(8,128)}, f32[2,64,32,256]{3,2,1,0:T(8,128)}, u32[]{:S(2)}, u32[]{:S(2)}) %collective-permute-start.3) | collective-permute-done | bytes 4194336 | tf_op jit(solution)/shard_map/ppermute | solution.py:24
  565.2 6.6 maximum_select_fusion.1
  571.9 7.5 collective-permute-done.4
  600.6 182.0 %collective-permute-done.5 = f32[2,64,32,256]{3,2,1,0:T(8,128)} collective-permute-done((f32[2,64,32,256]{3,2,1,0:T(8,128)}, f32[2,64,32,256]{3,2,1,0:T(8,128)}, u32[]{:S(2)}, u32[]{:S(2)}) %collective-permute-start.5) | collective-permute-done | bytes 4194336 | tf_op jit(solution)/shard_map/ppermute | solution.py:24
  786.6 7.2 maximum_select_fusion.3
  795.3 91.3 %collective-permute-done.6 = f32[2,64,32,256]{3,2,1,0:T(8,128)} collective-permute-done((f32[2,64,32,256]{3,2,1,0:T(8,128)}, f32[2,64,32,256]{3,2,1,0:T(8,128)}, u32[]{:S(2)}, u32[]{:S(2)}) %collective-permute-start.6) | collective-permute-done | bytes 4194336 | tf_op jit(solution)/shard_map/ppermute | solution.py:24
  925.3 91.4 %collective-permute-done.7 = f32[2,64,32,256]{3,2,1,0:T(8,128)S(1)} collective-permute-done((f32[2,64,32,256]{3,2,1,0:T(8,128)S(1)}, f32[2,64,32,256]{3,2,1,0:T(8,128)S(1)}, u32[]{:S(2)}, u32[]{:S(2)}) %collective-permute-start.7) | collective-permute-done | bytes 4194336 | tf_op jit(solution)/shard_map/ppermute | solution.py:24
  1022.2 179.9 %collective-permute-done.8 = f32[2,64,32,256]{3,2,1,0:T(8,128)S(1)} collective-permute-done((f32[2,64,32,256]{3,2,1,0:T(8,128)S(1)}, f32[2,64,32,256]{3,2,1,0:T(8,128)S(1)}, u32[]{:S(2)}, u32[]{:S(2)}) %collective-permute-start.8) | collective-permute-done | bytes 4194336 | tf_op jit(solution)/shard_map/ppermute | solution.py:24
  1215.2 7.1 collective-permute-done.9
  1228.0 90.9 %collective-permute-done.10 = f32[2,64,32,256]{3,2,1,0:T(8,128)S(1)} collective-permute-done((f32[2,64,32,256]{3,2,1,0:T(8,128)S(1)}, f32[2,64,32,256]{3,2,1,0:T(8,128)S(1)}, u32[]{:S(2)}, u32[]{:S(2)}) %collective-permute-start.10) | collective-permute-done | bytes 4194336 | tf_op jit(solution)/shard_map/ppermute | solution.py:24
  1325.7 90.0 %collective-permute-done.11 = f32[2,64,32,256]{3,2,1,0:T(8,128)S(1)} collective-permute-done((f32[2,64,32,256]{3,2,1,0:T(8,128)S(1)}, f32[2,64,32,256]{3,2,1,0:T(8,128)S(1)}, u32[]{:S(2)}, u32[]{:S(2)}) %collective-permute-start.11) | collective-permute-done | bytes 4194336 | tf_op jit(solution)/shard_map/ppermute | solution.py:24
  1442.4 582.9 %while.38 = (s32[]{:T(128)}, f32[12,3,512]{2,1,0:T(4,128)S(1)}, f32[12,512]{1,0:T(8,128)}, f32[12,69,512]{2,1,0:T(8,128)}, f32[12,37,512]{2,1,0:T(8,128)}, /*ind...) while((s32[]{:T(128)}, f32[12,3,512]{2,1,0:T(4,128)S(1)}, ...), condition=%wide.region_10.11_spmd, body=%wide.region_6.10_spmd.sunk | while | flops 12059120640 | bytes 75082880 | solution.py:311
  1444.3 6.5 broadcast_multiply_fusion.7
  1469.0 19.1 fusion.392
  1492.9 6.5 broadcast_multiply_fusion.7
  1517.6 19.1 fusion.392
  1541.5 6.5 broadcast_multiply_fusion.7
  1566.2 19.1 fusion.392
  1590.0 6.5 broadcast_multiply_fusion.7
  1614.8 19.1 fusion.392
  1638.6 6.5 broadcast_multiply_fusion.7
  1663.3 19.1 fusion.392
  1687.2 6.5 broadcast_multiply_fusion.7
  1711.9 19.1 fusion.392
  1735.8 6.5 broadcast_multiply_fusion.7
  1760.5 19.1 fusion.392
  1784.3 6.5 broadcast_multiply_fusion.7
  1809.1 19.1 fusion.392
  1857.6 19.1 fusion.392
  1906.2 19.1 fusion.392
  1954.8 19.1 fusion.392
  2003.3 19.1 fusion.392
  (631 shorter events, 697.9 us)
Async XLA Ops:
  1.6 0.8 copy-start.17
  3.1 2.5 copy-start.15
  7.1 11.1 all-to-all-start
  341.9 8.5 collective-permute-start
  350.5 9.7 collective-permute-start.1
  366.2 2.6 copy-start.3
  368.8 90.1 %collective-permute-start.2 = (f32[2,64,32,256]{3,2,1,0:T(8,128)}, f32[2,64,32,256]{3,2,1,0:T(8,128)}, u32[]{:S(2)}, u32[]{:S(2)}) collective-permute-start(f32[2,64,32,256]{3,2,1,0:T(8,128)} %pad_maximum_fusion), channel_id=1, source_target_pairs={{0,4},{4,0},{1,5},{5,1},{2,6},{6,2},{3,7},{7,3},{8,12},{12,8},{9,1... | collective-permute-start | bytes 12582920 | tf_op jit(solution)/shard_map/ppermute | solution.py:24
  369.6 93.3 %copy-start.4 = (f32[2048,256]{1,0:T(8,128)S(1)}, f32[2048,256]{1,0:T(8,128)}, u32[]{:S(2)}) copy-start(f32[2048,256]{1,0:T(8,128)} %copy-done.3) | copy-start | bytes 6291460
  462.8 7.2 copy-start.10
  462.9 7.2 copy-start.12
  470.1 90.6 %collective-permute-start.3 = (f32[2,64,32,256]{3,2,1,0:T(8,128)}, f32[2,64,32,256]{3,2,1,0:T(8,128)}, u32[]{:S(2)}, u32[]{:S(2)}) collective-permute-start(f32[2,64,32,256]{3,2,1,0:T(8,128)} %maximum_select_fusion), channel_id=1, source_target_pairs={{0,2},{2,0},{1,3},{3,1},{4,6},{6,4},{5,7},{7,5},{8,10},{10,8},{9,1... | collective-permute-start | bytes 12582920 | tf_op jit(solution)/shard_map/ppermute | solution.py:24
  471.6 93.5 %copy-start.5 = (f32[2048,256]{1,0:T(8,128)S(1)}, f32[2048,256]{1,0:T(8,128)}, u32[]{:S(2)}) copy-start(f32[2048,256]{1,0:T(8,128)} %copy-done.3) | copy-start | bytes 6291460
  471.7 93.5 %copy-start.11 = (f32[1,64,32,256]{3,2,1,0:T(8,128)S(1)}, f32[1,64,32,256]{3,2,1,0:T(8,128)}, u32[]{:S(2)}) copy-start(f32[1,64,32,256]{3,2,1,0:T(8,128)} %copy-done.10) | copy-start | bytes 6291460
  471.7 93.5 %copy-start.13 = (f32[1,64,32,256]{3,2,1,0:T(8,128)S(1)}, f32[1,64,32,256]{3,2,1,0:T(8,128)}, u32[]{:S(2)}) copy-start(f32[1,64,32,256]{3,2,1,0:T(8,128)} %copy-done.12) | copy-start | bytes 6291460
  571.8 7.6 collective-permute-start.4
  597.0 2.6 copy-start
  599.7 182.9 %collective-permute-start.5 = (f32[2,64,32,256]{3,2,1,0:T(8,128)}, f32[2,64,32,256]{3,2,1,0:T(8,128)}, u32[]{:S(2)}, u32[]{:S(2)}) collective-permute-start(f32[2,64,32,256]{3,2,1,0:T(8,128)} %pad_maximum_fusion.1), channel_id=1, source_target_pairs={{0,16},{16,0},{8,24},{24,8},{1,17},{17,1},{9,25},{25,9},{2,18},{18... | collective-permute-start | bytes 12582920 | tf_op jit(solution)/shard_map/ppermute | solution.py:24
  600.6 186.0 %copy-start.1 = (f32[64,256,32]{1,2,0:T(8,128)S(1)}, f32[64,256,32]{1,2,0:T(8,128)}, u32[]{:S(2)}) copy-start(f32[64,256,32]{1,2,0:T(8,128)} %copy-done) | copy-start | bytes 6291460
  786.6 7.2 copy-start.6
  786.6 7.2 copy-start.8
  793.8 92.8 %collective-permute-start.6 = (f32[2,64,32,256]{3,2,1,0:T(8,128)}, f32[2,64,32,256]{3,2,1,0:T(8,128)}, u32[]{:S(2)}, u32[]{:S(2)}) collective-permute-start(f32[2,64,32,256]{3,2,1,0:T(8,128)} %maximum_select_fusion.3), channel_id=1, source_target_pairs={{0,8},{8,0},{16,24},{24,16},{1,9},{9,1},{17,25},{25,17},{2,10},{10... | collective-permute-start | bytes 12582920 | tf_op jit(solution)/shard_map/ppermute | solution.py:24
  795.3 95.8 %copy-start.2 = (f32[64,256,32]{1,2,0:T(8,128)S(1)}, f32[64,256,32]{1,2,0:T(8,128)}, u32[]{:S(2)}) copy-start(f32[64,256,32]{1,2,0:T(8,128)} %copy-done) | copy-start | bytes 6291460
  795.3 95.8 %copy-start.7 = (f32[1,64,32,256]{3,2,1,0:T(8,128)S(1)}, f32[1,64,32,256]{3,2,1,0:T(8,128)}, u32[]{:S(2)}) copy-start(f32[1,64,32,256]{3,2,1,0:T(8,128)} %copy-done.6) | copy-start | bytes 6291460
  795.3 95.8 %copy-start.9 = (f32[1,64,32,256]{3,2,1,0:T(8,128)S(1)}, f32[1,64,32,256]{3,2,1,0:T(8,128)}, u32[]{:S(2)}) copy-start(f32[1,64,32,256]{3,2,1,0:T(8,128)} %copy-done.8) | copy-start | bytes 6291460
  925.0 91.7 %collective-permute-start.7 = (f32[2,64,32,256]{3,2,1,0:T(8,128)S(1)}, f32[2,64,32,256]{3,2,1,0:T(8,128)S(1)}, u32[]{:S(2)}, u32[]{:S(2)}) collective-permute-start(f32[2,64,32,256]{3,2,1,0:T(8,128)S(1)} %maximum_select_fusion.5), channel_id=1, source_target_pairs={{0,8},{8,0},{16,24},{24,16},{1,9},{9,1},{17,25},{25,17},{2,10},{10... | collective-permute-start | bytes 12582920 | tf_op jit(solution)/shard_map/ppermute | solution.py:24
  1020.5 181.6 %collective-permute-start.8 = (f32[2,64,32,256]{3,2,1,0:T(8,128)S(1)}, f32[2,64,32,256]{3,2,1,0:T(8,128)S(1)}, u32[]{:S(2)}, u32[]{:S(2)}) collective-permute-start(f32[2,64,32,256]{3,2,1,0:T(8,128)S(1)} %maximum_select_fusion.6), channel_id=1, source_target_pairs={{0,16},{16,0},{8,24},{24,8},{1,17},{17,1},{9,25},{25,9},{2,18},{18... | collective-permute-start | bytes 12582920 | tf_op jit(solution)/shard_map/ppermute | solution.py:24
  1215.1 7.2 collective-permute-start.9
  1226.2 92.7 %collective-permute-start.10 = (f32[2,64,32,256]{3,2,1,0:T(8,128)S(1)}, f32[2,64,32,256]{3,2,1,0:T(8,128)S(1)}, u32[]{:S(2)}, u32[]{:S(2)}) collective-permute-start(f32[2,64,32,256]{3,2,1,0:T(8,128)S(1)} %maximum_select_fusion.8), channel_id=1, source_target_pairs={{0,2},{2,0},{1,3},{3,1},{4,6},{6,4},{5,7},{7,5},{8,10},{10,8},{9,1... | collective-permute-start | bytes 12582920 | tf_op jit(solution)/shard_map/ppermute | solution.py:24
  1323.2 92.5 %collective-permute-start.11 = (f32[2,64,32,256]{3,2,1,0:T(8,128)S(1)}, f32[2,64,32,256]{3,2,1,0:T(8,128)S(1)}, u32[]{:S(2)}, u32[]{:S(2)}) collective-permute-start(f32[2,64,32,256]{3,2,1,0:T(8,128)S(1)} %maximum_select_fusion.9), channel_id=1, source_target_pairs={{0,4},{4,0},{1,5},{5,1},{2,6},{6,2},{3,7},{7,3},{8,12},{12,8},{9,1... | collective-permute-start | bytes 12582920 | tf_op jit(solution)/shard_map/ppermute | solution.py:24
  1424.1 7.0 collective-permute-start.12
  1426.7 4.6 copy-start.14
  1426.7 4.6 copy-start.18
  1431.1 5.1 collective-permute-start.13
  1442.4 593.8 %copy-start.16 = (f32[32]{0:T(128)S(1)}, f32[32]{0:T(128)}, u32[]{:S(2)}) copy-start(f32[32]{0:T(128)} %copy-done.15) | copy-start | bytes 388
  2026.0 9.5 all-to-all-start.1
where the time goes:
time: 2050 us; the launch traced here: 2040 us
  waiting for transfers between devices  951 us (46%)
  matrix products  384 us (19%)
  local copies, waits for them, and re-layouts  366 us (18%)
  other arithmetic  309 us (15%)
  starting transfers between devices  23.1 us (1%)
    ppermute x10, waiting for transfers between devices, swapped(): return lax.ppermute(block, axis, route)  919 us
    dot_general x12, matrix products, pull(): sampled = jnp.einsum('cga,gz->caz', stacked, potential, precision=HIGHEST)  229 us
    dot_general x12, matrix products, deposit(): jnp.dot(outer_table, table_z * group[3][:, None], precision=HIGHEST)  105 us
    dynamic_update_slice x72, other arithmetic, per_device(): extended, stored = lax.scan(deposit, start_grid, grouped)  86.1 us
    mul x24, local copies, waits for them, and re-layouts, pull(): slope_x[:, None, :] * table_y[None, :, :]  85.2 us
    mul x24, local copies, waits for them, and re-layouts, pull(): table_x[:, None, :] * slope_y[None, :, :]  83.9 us
    mul x12, other arithmetic, pull(): table_x[:, None, :] * table_y[None, :, :]  78.3 us
    mul x12, local copies, waits for them, and re-layouts, deposit(): table_x[:, None, :] * table_y[None, :, :]  72.8 us
  transfers between devices with their start and end apart: 16, of which 16 were waited for; matrix products, arithmetic and copies ran while one was open for 0% of the time, Pallas kernels for 0%

commit v1 on v0

v1 whole, which is shorter than its diff:
```python
import math

import jax
import jax.numpy as jnp
import numpy as np
from jax import lax
from jax.experimental import pallas as pl
from jax.experimental.pallas import tpu as pltpu
from jax.sharding import PartitionSpec as P

K = 256
EWALD_GAIN = 4.0
EWALD_BETA = 0.6
SPLINE_SUMS = (1.0 / 120.0, 26.0 / 120.0, 66.0 / 120.0, 26.0 / 120.0, 1.0 / 120.0)
HIGHEST = lax.Precision.HIGHEST
HIGH = lax.Precision.HIGH
LANES = 128
ROWS_CHUNK = 14
GROUP_BLOCKS = 2


def hartley():
    steps = np.arange(K)
    angle = 2.0 * math.pi / K * (np.outer(steps, steps) % K)
    return (np.cos(angle) + np.sin(angle)).astype(np.float32)


def wave_profile():
    steps = np.arange(K)
    folded = np.where(2 * steps < K, steps, steps - K) / K
    waves = np.exp(2j * math.pi / K * np.outer(steps, np.arange(5)))
    modulus = 1.0 / np.abs(waves @ np.array(SPLINE_SUMS)) ** 2
    squared = folded * folded
    gauss = np.exp(-(math.pi * math.pi) * squared / (EWALD_BETA * EWALD_BETA))
    return squared.astype(np.float32), (gauss * modulus).astype(np.float32)


def from_behind(value, axis, steps):
    count = lax.axis_size(axis)
    pairs = [(source, (source + steps) % count) for source in range(count)]
    return lax.ppermute(value, axis, pairs)


def spline_six(u):
    older_values = [1.0 - u, u]
    slopes = []
    for spline_order in range(3, 7):
        newer_values = []
        for k in range(spline_order):
            terms = []
            if k >= 1:
                terms.append((u + (spline_order - 1 - k)) * older_values[k - 1])
            if k <= spline_order - 2:
                terms.append((k + 1 - u) * older_values[k])
            newer_values.append(sum(terms[1:], terms[0]) * (1.0 / (spline_order - 1)))
        if spline_order == 6:
            slopes = [-older_values[0]]
            slopes += [older_values[k - 1] - older_values[k] for k in range(1, 5)]
            slopes += [older_values[4]]
        older_values = newer_values
    return (older_values, slopes)


def placed(offset, values):
    table = jnp.zeros(offset.shape, jnp.float32)
    for k in range(6):
        table = jnp.where(offset == k, values[k], table)
    return table


def offsets(base, rows, wrap):
    width = base.shape[1]
    offset = lax.broadcasted_iota(jnp.int32, (rows, width), 0) - base
    return offset & (K - 1) if wrap else offset


def halves(value):
    upper = value.astype(jnp.bfloat16)
    lower = (value - upper.astype(jnp.float32)).astype(jnp.bfloat16)
    return upper, lower


def deposit_kernel(count_ref, atoms_ref, grid_ref):
    step = pl.program_id(0)
    rows, columns, depth = grid_ref.shape
    width = atoms_ref.shape[2]

    @pl.when(step == 0)
    def _():
        grid_ref[...] = jnp.zeros(grid_ref.shape, jnp.float32)

    @pl.when(step < count_ref[0])
    def _():
        atoms = atoms_ref[0]
        base = atoms.astype(jnp.int32)
        table_x = placed(offsets(base[4:5], rows, False), spline_six(atoms[0:1])[0])
        table_y = placed(offsets(base[5:6], columns, False), spline_six(atoms[1:2])[0])
        table_z = placed(offsets(base[6:7], depth, True), spline_six(atoms[2:3])[0])
        upper, lower = halves((table_z * atoms[3:4]).T)
        weights = jnp.concatenate([upper, lower, upper], axis=0)
        for start in range(0, rows, ROWS_CHUNK):
            chunk = table_x[start : start + ROWS_CHUNK]
            outer = (chunk[:, None, :] * table_y[None, :, :]).reshape(-1, width)
            upper, lower = halves(outer)
            spread = jnp.dot(
                jnp.concatenate([upper, upper, lower], axis=1),
                weights,
                preferred_element_type=jnp.float32,
            )
            grid_ref[start : start + ROWS_CHUNK] += spread.reshape(-1, columns, depth)


def pull_kernel(count_ref, atoms_ref, potential_ref, forces_ref, parts):
    step = pl.program_id(0)
    rows, columns, depth = potential_ref.shape
    width = atoms_ref.shape[2]
    piece = ROWS_CHUNK * columns

    @pl.when(step == 0)
    def _():
        for index in range(rows // ROWS_CHUNK):
            start = index * ROWS_CHUNK
            values = potential_ref[start : start + ROWS_CHUNK].reshape(piece, depth)
            upper, lower = halves(values)
            parts[index * piece : (index + 1) * piece] = jnp.concatenate(
                [upper, lower, upper], axis=1
            )

    @pl.when(step >= count_ref[0])
    def _():
        forces_ref[...] = jnp.zeros(forces_ref.shape, jnp.float32)

    @pl.when(step < count_ref[0])
    def _():
        atoms = atoms_ref[0]
        base = atoms.astype(jnp.int32)
        offset_x = offsets(base[4:5], rows, False)
        offset_y = offsets(base[5:6], columns, False)
        offset_z = offsets(base[6:7], depth, True)
        values, slopes = spline_six(atoms[0:1])
        table_x, slope_x = placed(offset_x, values), placed(offset_x, slopes)
        values, slopes = spline_six(atoms[1:2])
        table_y, slope_y = placed(offset_y, values), placed(offset_y, slopes)
        values, slopes = spline_six(atoms[2:3])
        both = jnp.concatenate([placed(offset_z, values), placed(offset_z, slopes)], axis=1)
        upper, lower = halves(both)
        weights = jnp.concatenate([upper, upper, lower], axis=0)
        totals = [jnp.zeros((8, width), jnp.float32) for _ in range(3)]
        for index in range(rows // ROWS_CHUNK):
            start = index * ROWS_CHUNK
            sampled = jnp.dot(
                parts[index * piece : (index + 1) * piece],
                weights,
                preferred_element_type=jnp.float32,
            ).reshape(ROWS_CHUNK, columns, 2 * width)
            for row in range(ROWS_CHUNK):
                plain = sampled[row, :, :width]
                sloped = sampled[row, :, width:]
                value_x = table_x[start + row : start + row + 1]
                turned_x = slope_x[start + row : start + row + 1]

                def folded(terms):
                    return jnp.sum(terms.reshape(columns // 8, 8, width), axis=0)

                totals[0] = totals[0] + turned_x * folded(plain * table_y)
                totals[1] = totals[1] + value_x * folded(plain * slope_y)
                totals[2] = totals[2] + value_x * folded(sloped * table_y)
        result = [-atoms[3:4] * jnp.sum(total, axis=0, keepdims=True) for total in totals]
        forces_ref[0] = jnp.concatenate(
            result + [jnp.zeros((5, width), jnp.float32)], axis=0
        )


def deposit(count, atoms, rows, columns):
    groups, lines, width = atoms.shape
    return pl.pallas_call(
        deposit_kernel,
        out_shape=jax.ShapeDtypeStruct((rows, columns, K), jnp.float32),
        grid=(groups,),
        in_specs=[
            pl.BlockSpec(memory_space=pltpu.SMEM),
            pl.BlockSpec((1, lines, width), lambda g: (g, 0, 0)),
        ],
        out_specs=pl.BlockSpec((rows, columns, K), lambda g: (0, 0, 0)),
        compiler_params=pltpu.CompilerParams(vmem_limit_bytes=48 * 2**20),
        name="deposit",
    )(count, atoms)


def pull(count, atoms, potential):
    groups, lines, width = atoms.shape
    rows, columns, _ = potential.shape
    return pl.pallas_call(
        pull_kernel,
        out_shape=jax.ShapeDtypeStruct((groups, lines, width), jnp.float32),
        grid=(groups,),
        in_specs=[
            pl.BlockSpec(memory_space=pltpu.SMEM),
            pl.BlockSpec((1, lines, width), lambda g: (g, 0, 0)),
            pl.BlockSpec((rows, columns, K), lambda g: (0, 0, 0)),
        ],
        out_specs=pl.BlockSpec((1, lines, width), lambda g: (g, 0, 0)),
        scratch_shapes=[pltpu.VMEM((rows * columns, 3 * K), jnp.bfloat16)],
        compiler_params=pltpu.CompilerParams(vmem_limit_bytes=48 * 2**20),
        name="pull",
    )(count, atoms, potential)


def transformed(grid, span_x, span_y, rows_dev, cols_dev):
    matrix = jnp.asarray(hartley())
    packed = LANES // span_y
    bands = span_x // packed
    span_z = K // cols_dev
    slab = span_z // rows_dev
    identity = jnp.eye(packed, dtype=jnp.float32)
    mixing = (
        matrix.reshape(cols_dev, 1, span_y, 1, K) * identity[None, :, None, :, None]
    ).reshape(cols_dev, packed * span_y, packed * K)

    spectrum = lax.dot_general(matrix, grid, (((1,), (1,)), ((), ())), precision=HIGH)
    spectrum = spectrum.reshape(cols_dev, span_z, bands, LANES)
    spectrum = lax.all_to_all(spectrum, "py", split_axis=0, concat_axis=0, tiled=True)
    spectrum = jnp.einsum("szbl,slk->zbk", spectrum, mixing, precision=HIGH)
    spectrum = spectrum.reshape(rows_dev, slab, span_x, K)
    spectrum = lax.all_to_all(spectrum, "px", split_axis=0, concat_axis=0, tiled=True)
    split = matrix.reshape(K, rows_dev, span_x)
    spectrum = jnp.einsum("ksx,szxy->zky", split, spectrum, precision=HIGH)

    squared, profile = (jnp.asarray(table) for table in wave_profile())
    first = lax.axis_index("py") * span_z + lax.axis_index("px") * slab
    squared_z = lax.dynamic_slice(squared, (first,), (slab,))
    profile_z = lax.dynamic_slice(profile, (first,), (slab,))
    total = squared_z[:, None, None] + squared[None, :, None] + squared[None, None, :]
    gain = profile_z[:, None, None] * profile[None, :, None] * profile[None, None, :]
    kernel = jnp.where(
        total > 0, (EWALD_GAIN / float(K**3)) * gain / jnp.where(total > 0, total, 1.0), 0.0
    )
    spectrum = spectrum * kernel

    spectrum = jnp.einsum("ksx,zky->szxy", split, spectrum, precision=HIGH)
    spectrum = lax.all_to_all(spectrum, "px", split_axis=0, concat_axis=0, tiled=True)
    spectrum = spectrum.reshape(span_z, bands, packed * K)
    spectrum = jnp.einsum("zbk,slk->szbl", spectrum, mixing, precision=HIGH)
    spectrum = lax.all_to_all(spectrum, "py", split_axis=0, concat_axis=0, tiled=True)
    spectrum = spectrum.reshape(K, span_x * span_y)
    return lax.dot_general(spectrum, matrix, (((0,), (0,)), ((), ())), precision=HIGH)


def per_device(fractions, charge, cell_index, destination, live_blocks):
    rows_dev = lax.axis_size("px")
    cols_dev = lax.axis_size("py")
    span_x = K // rows_dev
    span_y = K // cols_dev
    blocks, width = charge.shape
    capacity = max(2, 3 * blocks // (2 * cols_dev))
    slots = cols_dev * capacity
    padded = -(-slots // GROUP_BLOCKS) * GROUP_BLOCKS
    groups = padded // GROUP_BLOCKS
    rows = -(-(span_x + 5) // ROWS_CHUNK) * ROWS_CHUNK
    columns = -(-(span_y + 5) // 8) * 8

    alive = (jnp.arange(blocks, dtype=jnp.int32) < live_blocks[0]).astype(jnp.int32)
    target = destination[:, 0]
    matches = (target[:, None] == jnp.arange(cols_dev, dtype=jnp.int32)[None, :]).astype(jnp.int32)
    matches = matches * alive[:, None]
    earlier = jnp.cumsum(matches, axis=0) - matches
    position = jnp.sum(earlier * matches, axis=1)
    slot_of = jnp.where(alive > 0, target * capacity + position, -1)
    picked = (slot_of[None, :] == jnp.arange(slots, dtype=jnp.int32)[:, None]).astype(jnp.float32)
    payload = jnp.stack(
        [
            fractions[:, 0],
            fractions[:, 1],
            fractions[:, 2],
            charge,
            (cell_index // (span_y * K)).astype(jnp.float32),
            (cell_index // K % span_y).astype(jnp.float32),
            (cell_index % K).astype(jnp.float32),
            jnp.ones(charge.shape, jnp.float32),
        ],
        axis=1,
    )
    outgoing = jnp.dot(picked, payload.reshape(blocks, -1), precision=HIGHEST)
    outgoing = outgoing.reshape(cols_dev, capacity, 8, width)
    arrived = lax.all_to_all(outgoing, "py", split_axis=0, concat_axis=0, tiled=True)
    arrived = arrived.reshape(slots, 8, width)
    used = (arrived[:, 7, 0] > 0.5).astype(jnp.int32)
    place = jnp.where(used > 0, jnp.cumsum(used) - used, -1)
    chosen = (place[None, :] == jnp.arange(padded, dtype=jnp.int32)[:, None]).astype(jnp.float32)
    atoms = jnp.dot(chosen, arrived.reshape(slots, -1), precision=HIGHEST)
    atoms = (
        atoms.reshape(groups, GROUP_BLOCKS, 8, width)
        .transpose(0, 2, 1, 3)
        .reshape(groups, 8, GROUP_BLOCKS * width)
    )
    count = ((jnp.sum(used) + GROUP_BLOCKS - 1) // GROUP_BLOCKS).reshape(1)

    extended = deposit(count, atoms, rows, columns)
    moved_rows = from_behind(extended[span_x : span_x + 5], "px", 1)
    extended = jnp.concatenate([extended[:5] + moved_rows, extended[5:span_x]], axis=0)
    moved_cols = from_behind(extended[:, span_y : span_y + 5], "py", 1)
    grid = jnp.concatenate([extended[:, :5] + moved_cols, extended[:, 5:span_y]], axis=1)

    potential = transformed(
        grid.reshape(span_x * span_y, K), span_x, span_y, rows_dev, cols_dev
    ).reshape(span_x, span_y, K)
    lower_rows = from_behind(potential[:5], "px", -1)
    potential = jnp.concatenate([potential, lower_rows], axis=0)
    lower_cols = from_behind(potential[:, :5], "py", -1)
    potential = jnp.concatenate([potential, lower_cols], axis=1)
    potential = jnp.pad(
        potential, ((0, rows - span_x - 5), (0, columns - span_y - 5), (0, 0))
    )

    forces = pull(count, atoms, potential)[:, :3]
    forces = (
        forces.reshape(groups, 3, GROUP_BLOCKS, width)
        .transpose(0, 2, 1, 3)
        .reshape(padded, 3 * width)
    )
    forces = lax.dot_general(chosen, forces, (((0,), (0,)), ((), ())), precision=HIGHEST)
    returned = lax.all_to_all(
        forces.reshape(cols_dev, capacity, 3, width), "py", split_axis=0, concat_axis=0, tiled=True
    ).reshape(slots, 3 * width)
    result = lax.dot_general(picked, returned, (((0,), (0,)), ((), ())), precision=HIGHEST)
    return result.reshape(blocks, 3, width)


def solution(mesh):
    split = (
        P(("px", "py"), None, None),
        P(("px", "py"), None),
        P(("px", "py"), None),
        P(("px", "py"), None),
        P(("px", "py")),
    )
    return jax.shard_map(
        per_device,
        mesh=mesh,
        in_specs=split,
        out_specs=P(("px", "py"), None, None),
        check_vma=False,
    )
```

time: 2050 us -> 332 us (0.16)
  waiting for transfers between devices: 951 us -> 134 us
  matrix products: 384 us -> 22.5 us
  local copies, waits for them, and re-layouts: 366 us -> 27.5 us
  other arithmetic: 309 us -> 10.1 us
  blocking collectives: 0 us -> 64.8 us
  Pallas kernels: 0 us -> 38.7 us
    ppermute x10 -> x0, waiting for transfers between devices: 919 us -> none  [swapped(): return lax.ppermute(block, axis, route)]
    dot_general x44 -> x10, matrix products: 384 us -> 22.5 us  [the longest x1 7.83 us: transformed(): spectrum = jnp.einsum('zbk,slk->szbl', spectrum, mixing, precision=HIGH)]
    mul x73 -> x4, local copies, waits for them, and re-layouts: 315 us -> 14.6 us  [transformed(): matrix.reshape(cols_dev, 1, span_y, 1, K) * identity[None, :, None, :, None]]
    mul x44 -> x3, other arithmetic: 129 us -> 3.8 us  [the longest x1 3 us: transformed(): matrix.reshape(cols_dev, 1, span_y, 1, K) * identity[None, :, None, :, None]]
    all_to_all x1 -> x3, waiting for transfers between devices: 5.19 us -> 102 us  [the longest x2 84.1 us: transformed(): lax.all_to_all(spectrum, 'px', split_axis=0, concat_axis=0, tiled=True)]
    dynamic_update_slice x84 -> x0, other arithmetic: 86.4 us -> none  [the longest x72 86.1 us: per_device(): extended, stored = lax.scan(deposit, start_grid, grouped)]
    all_to_all x0 -> x2, blocking collectives: none -> 64.8 us  [the longest x1 33.4 us: per_device(): lax.all_to_all(forces.reshape(cols_dev, capacity, 3, width), 'py', split_...]
    select_n x40 -> x3, other arithmetic: 47 us -> 0.68 us  [the longest x1 0.66 us: per_device(): slot_of = jnp.where(alive > 0, target * capacity + position, -1)]
  transfers between devices with their start and end apart: 16 -> 8, of which waited for: 16 -> 8; matrix products, arithmetic and copies ran while one was open for 0% -> 6% of each run, Pallas kernels for 0% -> 0%
where the time goes in v1:
time: 332 us; the launch traced here: 330 us
  waiting for transfers between devices  134 us (40%)
  blocking collectives  64.8 us (20%)
  Pallas kernels  38.7 us (12%)
  starting transfers between devices  30.3 us (9%)
  local copies, waits for them, and re-layouts  27.5 us (8%)
  matrix products  22.5 us (7%)
  other arithmetic  10.1 us (3%)
    all_to_all x2, waiting for transfers between devices, transformed(): lax.all_to_all(spectrum, 'px', split_axis=0, concat_axis=0, tiled=True)  84.1 us
    all_to_all x1, blocking collectives, per_device(): lax.all_to_all(forces.reshape(cols_dev, capacity, 3, width), 'py', split_...  33.4 us
    all_to_all x1, blocking collectives, transformed(): lax.all_to_all(spectrum, 'py', split_axis=0, concat_axis=0, tiled=True)  31.4 us
    ppermute x4, waiting for transfers between devices, from_behind(): return lax.ppermute(value, axis, pairs)  26.1 us
    pallas_call x1, Pallas kernels, pull(): pl.pallas_call(pull_kernel, out_shape=jax.ShapeDtypeStruct((groups, lines...  24.4 us
    all_to_all x1, waiting for transfers between devices, transformed(): lax.all_to_all(spectrum, 'py', split_axis=0, concat_axis=0, tiled=True)  17.7 us
    mul x4, local copies, waits for them, and re-layouts, transformed(): matrix.reshape(cols_dev, 1, span_y, 1, K) * identity[None, :, None, :, None]  14.6 us
    pallas_call x1, Pallas kernels, deposit(): pl.pallas_call(deposit_kernel, out_shape=jax.ShapeDtypeStruct((rows, colu...  14.3 us
  transfers between devices with their start and end apart: 8, of which 8 were waited for; matrix products, arithmetic and copies ran while one was open for 6% of the time, Pallas kernels for 0%

profile of v1, /device:TPU:0, one launch (start us, length us, event | category | flops | bytes accessed | tf_op | source)
XLA Modules:
  0.0 329.7 jit_solution(12168928023930997962)
XLA Ops:
  0.7 0.7 fusion.66
  1.5 0.8 fusion.54
  2.3 0.8 constant_dynamic-update-slice_fusion.1
  3.1 0.7 bitcast_dynamic-update-slice_fusion
  3.8 0.7 fusion.58
  4.6 0.7 fusion.62
  5.3 0.7 fusion.65
  6.0 0.7 compare_select_fusion.1
  7.0 0.7 copy.50
  7.7 5.2 %all-to-all-start = ((f32[8,6,8,128]{3,2,1,0:T(8,128)}), f32[8,6,8,128]{3,2,1,0:T(8,128)S(1)}, u32[]{:S(2)}, u32[]{:S(2)}) async-start(f32[8,6,8,128]{3,2,1,0:T(8,128)} %copy.50), calls=%async_computation | async-start | bytes 393216 | tf_op jit(solution)/shard_map/all_to_all | solution.py:285
  12.9 6.2 %all-to-all-done = f32[8,6,8,128]{3,2,1,0:T(8,128)S(1)} async-done(((f32[8,6,8,128]{3,2,1,0:T(8,128)}), f32[8,6,8,128]{3,2,1,0:T(8,128)S(1)}, u32[]{:S(2)}, u32[]{:S(2)}) %all-to-all-start) | async-done | bytes 196640 | tf_op jit(solution)/shard_map/all_to_all | solution.py:285
  19.1 1.5 fusion.81
  21.8 14.3 %deposit.1 = f32[70,40,256]{2,1,0:T(8,128)S(1)} custom-call(s32[1]{0:T(128)} %bitcast.16.count_ref, f32[24,8,256]{2,1,0:T(8,128)S(1)} %bitcast.182), custom_call_target="tpu_custom_call" | custom-call | tf_op jit(solution)/shard_map/deposit/pallas_call | solution.py:176
  36.2 1.6 collective-permute-start
  38.0 5.8 %collective-permute-done = f32[5,40,256]{2,1,0:T(8,128)S(1)} collective-permute-done((f32[5,40,256]{2,1,0:T(8,128)S(1)}, f32[5,40,256]{2,1,0:T(8,128)S(1)}, u32[]{:S(2)}, u32[]{:S(2)}) %collective-permute-start) | collective-permute-done | bytes 204832 | tf_op jit(solution)/shard_map/ppermute | solution.py:41
  43.9 11.6 %collective-permute-done.1 = f32[64,5,256]{2,1,0:T(8,128)S(1)} collective-permute-done((f32[64,5,256]{2,1,0:T(8,128)S(1)}, f32[64,5,256]{2,1,0:T(8,128)S(1)}, u32[]{:S(2)}, u32[]{:S(2)}) %collective-permute-start.1) | collective-permute-done | bytes 327712 | tf_op jit(solution)/shard_map/ppermute | solution.py:41
  55.7 0.3 fusion.15
  56.0 0.6 copy-done
  56.6 1.1 convolution_bitcast_fusion
  57.7 1.7 copy.85
  59.4 14.1 %all-to-all-start.1 = ((f32[8,32,16,128]{3,2,1,0:T(8,128)}), f32[8,32,16,128]{3,2,1,0:T(8,128)S(1)}, u32[]{:S(2)}, u32[]{:S(2)}) async-start(f32[8,32,16,128]{3,2,1,0:T(8,128)} %bitcast.186), calls=%async_computation.1 | async-start | bytes 4194304 | tf_op jit(solution)/shard_map/all_to_all | solution.py:222
  73.5 2.9 mul.108
  76.5 5.8 %mul.112 = f32[8,128,1024]{2,1,0:T(8,128)} reshape(f32[8,4,32,4,256]{4,3,2,1,0:T(4,128)} %mul.108) | data formatting | bytes 8388608 | tf_op jit(solution)/shard_map/mul | solution.py:217
  82.5 17.7 %all-to-all-done.1 = f32[8,32,16,128]{3,2,1,0:T(8,128)S(1)} async-done(((f32[8,32,16,128]{3,2,1,0:T(8,128)}), f32[8,32,16,128]{3,2,1,0:T(8,128)S(1)}, u32[]{:S(2)}, u32[]{:S(2)}) %all-to-all-start.1) | async-done | bytes 2097184 | tf_op jit(solution)/shard_map/all_to_all | solution.py:222
  100.2 6.4 %fusion.30 = f32[32,16,1024]{2,1,0:T(8,128)} fusion(f32[8,32,16,128]{3,2,1,0:T(8,128)S(1)} %all-to-all-done.1, f32[8,128,1024]{2,1,0:T(8,128)} %mul.112, f32[128,1024]{1,0:T(8,128)S(1)} %bitcast.189), kind=kOutput, calls=%fused_computation.31 | convolution fusion | flops 3222274048 | bytes 8912896 | tf_op jit(solution)/shard_map/szbl,slk->zbk/dot_general | solution.py:223
  106.5 2.9 reshape.280
  109.4 3.9 %all-to-all-start.2 = ((f32[4,8,64,256]{3,2,1,0:T(8,128)}), f32[4,8,64,256]{3,2,1,0:T(8,128)S(1)}, u32[]{:S(2)}, u32[]{:S(2)}) async-start(f32[4,8,64,256]{3,2,1,0:T(8,128)} %reshape.280), calls=%async_computation.2 | async-start | bytes 4194304 | tf_op jit(solution)/shard_map/all_to_all | solution.py:225
  113.6 45.2 %all-to-all-done.2 = f32[4,8,64,256]{3,2,1,0:T(8,128)S(1)} async-done(((f32[4,8,64,256]{3,2,1,0:T(8,128)}), f32[4,8,64,256]{3,2,1,0:T(8,128)S(1)}, u32[]{:S(2)}, u32[]{:S(2)}) %all-to-all-start.2) | async-done | bytes 2097184 | tf_op jit(solution)/shard_map/all_to_all | solution.py:225
  158.9 1.8 fusion.82
  160.7 1.7 fusion.22
  162.4 1.5 copy.57
  163.9 3.6 %all-to-all-start.3 = ((f32[4,8,64,256]{3,2,1,0:T(8,128)}), f32[4,8,64,256]{3,2,1,0:T(8,128)S(1)}, u32[]{:S(2)}, u32[]{:S(2)}) async-start(f32[4,8,64,256]{3,2,1,0:T(8,128)} %copy.57), calls=%async_computation.3 | async-start | bytes 4194304 | tf_op jit(solution)/shard_map/all_to_all | solution.py:241
  167.5 3.0 broadcast_multiply_fusion
  170.5 5.8 %reshape.299 = f32[8,128,1024,1]{2,1,0,3:T(8,128)} reshape(f32[8,4,32,4,256]{4,3,2,1,0:T(4,128)} %broadcast_multiply_fusion) | data formatting | bytes 8388608 | tf_op jit(solution)/shard_map/mul | solution.py:217
  176.3 38.9 %all-to-all-done.3 = f32[4,8,64,256]{3,2,1,0:T(8,128)S(1)} async-done(((f32[4,8,64,256]{3,2,1,0:T(8,128)}), f32[4,8,64,256]{3,2,1,0:T(8,128)S(1)}, u32[]{:S(2)}, u32[]{:S(2)}) %all-to-all-start.3) | async-done | bytes 2097184 | tf_op jit(solution)/shard_map/all_to_all | solution.py:241
  215.2 1.6 reshape.282
  216.8 7.8 %fusion.25 = f32[8,32,16,128]{3,1,2,0:T(8,128)S(1)} fusion(f32[32,16,1024]{2,1,0:T(8,128)} %reshape.282, f32[8,128,1024,1]{2,1,0,3:T(8,128)} %reshape.299), kind=kOutput, calls=%fused_computation.30 | convolution fusion | flops 3221225472 | bytes 8388608 | tf_op jit(solution)/shard_map/zbk,slk->szbl/dot_general | solution.py:243
  224.6 31.4 %all_to_all.30 = f32[8,32,16,128]{3,1,2,0:T(8,128)S(1)} all-to-all(f32[8,32,16,128]{3,1,2,0:T(8,128)S(1)} %fusion.25), channel_id=1, replica_groups=mesh['px'=4,'py'=8] {'py'}, dimensions={0} | all-to-all | bytes 4194304 | tf_op jit(solution)/shard_map/all_to_all | solution.py:244
  256.0 1.2 copy.59
  257.2 2.1 fusion.12
  259.3 1.5 collective-permute-start.2
  260.9 3.9 %collective-permute-done.2 = f32[5,32,256]{2,1,0:T(8,128)S(1)} collective-permute-done((f32[5,32,256]{2,1,0:T(8,128)S(1)}, f32[5,32,256]{2,1,0:T(8,128)S(1)}, u32[]{:S(2)}, u32[]{:S(2)}) %collective-permute-start.2) | collective-permute-done | bytes 163872 | tf_op jit(solution)/shard_map/ppermute | solution.py:41
  264.9 0.3 collective-permute-start.3
  265.4 4.8 %collective-permute-done.3 = f32[69,5,256]{2,0,1:T(8,128)S(1)} collective-permute-done((f32[69,5,256]{2,0,1:T(8,128)S(1)}, f32[69,5,256]{2,0,1:T(8,128)S(1)}, u32[]{:S(2)}, u32[]{:S(2)}) %collective-permute-start.3) | collective-permute-done | bytes 353312 | tf_op jit(solution)/shard_map/ppermute | solution.py:41
  270.3 0.3 select_maximum_fusion.potential_ref
  270.6 24.4 %pull.1 = f32[24,8,256]{2,1,0:T(8,128)S(1)} custom-call(s32[1]{0:T(128)} %bitcast.16.count_ref, f32[24,8,256]{2,1,0:T(8,128)S(1)} %bitcast.183, f32[70,40,256]{2,1,0:T(8,128)S(1)} %select_maximum_fusion.potential_ref), custom_call_target="tpu_custom_call" | custom-call | tf_op jit(solution)/shard_map/pull/pallas_call | solution.py:193
  295.5 33.4 %all_to_all.31 = f32[8,6,3,128]{3,2,1,0:T(4,128)S(1)} all-to-all(f32[8,6,3,128]{3,2,1,0:T(4,128)S(1)} %copy.65), channel_id=1, replica_groups=mesh['px'=4,'py'=8] {'py'}, dimensions={0} | all-to-all | bytes 147456 | tf_op jit(solution)/shard_map/all_to_all | solution.py:322
  328.9 0.8 fusion.43
  (47 shorter events, 2.7 us)
Async XLA Ops:
  7.7 11.4 %all-to-all-start = ((f32[8,6,8,128]{3,2,1,0:T(8,128)}), f32[8,6,8,128]{3,2,1,0:T(8,128)S(1)}, u32[]{:S(2)}, u32[]{:S(2)}) async-start(f32[8,6,8,128]{3,2,1,0:T(8,128)} %copy.50), calls=%async_computation | async-start | bytes 393216 | tf_op jit(solution)/shard_map/all_to_all | solution.py:285
  36.2 7.6 %collective-permute-start = (f32[5,40,256]{2,1,0:T(8,128)S(1)}, f32[5,40,256]{2,1,0:T(8,128)S(1)}, u32[]{:S(2)}, u32[]{:S(2)}) collective-permute-start(f32[5,40,256]{2,1,0:T(8,128)S(1)} %slice.50), channel_id=1, source_target_pairs={{0,8},{8,16},{16,24},{24,0},{1,9},{9,17},{17,25},{25,1},{2,10},{10... | collective-permute-start | bytes 614408 | tf_op jit(solution)/shard_map/ppermute | solution.py:41
  43.8 11.7 %collective-permute-start.1 = (f32[64,5,256]{2,1,0:T(8,128)S(1)}, f32[64,5,256]{2,1,0:T(8,128)S(1)}, u32[]{:S(2)}, u32[]{:S(2)}) collective-permute-start(f32[64,5,256]{2,1,0:T(8,128)S(1)} %pad_maximum_fusion.1), channel_id=1, source_target_pairs={{0,1},{1,2},{2,3},{3,4},{4,5},{5,6},{6,7},{7,0},{8,9},{9,10},{10,1... | collective-permute-start | bytes 983048 | tf_op jit(solution)/shard_map/ppermute | solution.py:41
  55.6 1.0 copy-start
  59.4 14.1 %copy-start.1 = (f32[8,32,256]{2,1,0:T(8,128)S(1)}, f32[8,32,256]{2,1,0:T(8,128)}, u32[]{:S(2)}) copy-start(f32[8,32,256]{2,1,0:T(8,128)} %constant.112) | copy-start | bytes 786436
  59.4 40.7 %all-to-all-start.1 = ((f32[8,32,16,128]{3,2,1,0:T(8,128)}), f32[8,32,16,128]{3,2,1,0:T(8,128)S(1)}, u32[]{:S(2)}, u32[]{:S(2)}) async-start(f32[8,32,16,128]{3,2,1,0:T(8,128)} %bitcast.186), calls=%async_computation.1 | async-start | bytes 4194304 | tf_op jit(solution)/shard_map/all_to_all | solution.py:222
  109.4 3.9 %copy-start.3 = (f32[256]{0:T(256)S(1)}, f32[256]{0:T(256)}, u32[]{:S(2)}) copy-start(f32[256]{0:T(256)} %constant.108.clone) | copy-start | bytes 3076
  109.4 4.0 %copy-start.4 = (f32[256]{0:T(256)S(1)}, f32[256]{0:T(256)}, u32[]{:S(2)}) copy-start(f32[256]{0:T(256)} %constant.107.clone) | copy-start | bytes 3076
  109.4 49.4 %copy-start.2 = (f32[256,4,64,1]{0,2,3,1:T(8,128)S(1)}, f32[256,4,64,1]{0,2,3,1:T(8,128)}, u32[]{:S(2)}) copy-start(f32[256,4,64,1]{0,2,3,1:T(8,128)} %constant.114) | copy-start | bytes 786436
  109.4 49.4 %all-to-all-start.2 = ((f32[4,8,64,256]{3,2,1,0:T(8,128)}), f32[4,8,64,256]{3,2,1,0:T(8,128)S(1)}, u32[]{:S(2)}, u32[]{:S(2)}) async-start(f32[4,8,64,256]{3,2,1,0:T(8,128)} %reshape.280), calls=%async_computation.2 | async-start | bytes 4194304 | tf_op jit(solution)/shard_map/all_to_all | solution.py:225
  158.8 1.9 copy-start.5
  163.9 51.3 %all-to-all-start.3 = ((f32[4,8,64,256]{3,2,1,0:T(8,128)}), f32[4,8,64,256]{3,2,1,0:T(8,128)S(1)}, u32[]{:S(2)}, u32[]{:S(2)}) async-start(f32[4,8,64,256]{3,2,1,0:T(8,128)} %copy.57), calls=%async_computation.3 | async-start | bytes 4194304 | tf_op jit(solution)/shard_map/all_to_all | solution.py:241
  259.3 5.4 %collective-permute-start.2 = (f32[5,32,256]{2,1,0:T(8,128)S(1)}, f32[5,32,256]{2,1,0:T(8,128)S(1)}, u32[]{:S(2)}, u32[]{:S(2)}) collective-permute-start(f32[5,32,256]{2,1,0:T(8,128)S(1)} %bitcast.196), channel_id=1, source_target_pairs={{0,24},{8,0},{16,8},{24,16},{1,25},{9,1},{17,9},{25,17},{2,26},{10... | collective-permute-start | bytes 491528 | tf_op jit(solution)/shard_map/ppermute | solution.py:41
  264.9 5.3 %collective-permute-start.3 = (f32[69,5,256]{2,0,1:T(8,128)S(1)}, f32[69,5,256]{2,0,1:T(8,128)S(1)}, u32[]{:S(2)}, u32[]{:S(2)}) collective-permute-start(f32[69,5,256]{2,0,1:T(8,128)S(1)} %copy.60), channel_id=1, source_target_pairs={{0,7},{1,0},{2,1},{3,2},{4,3},{5,4},{6,5},{7,6},{8,15},{9,8},{10,9... | collective-permute-start | bytes 1059848 | tf_op jit(solution)/shard_map/ppermute | solution.py:41
